TPU v7x, 32 devices: a whole 2x2x4 slice. The times are simulated.
32 devices in a mesh: region: 4 (over x, core), sector: 8 (over z, y).
Axes of the slice: x: 2, y: 2, z: 4, core: 2. Of those that a mesh axis runs over, the one named last changes fastest.
Arguments:
- psi: bfloat16 [4, 8, 256, 256], P('region', 'sector'), may hold values from -12 to 12
- left_env: bfloat16 [4, 8, 18, 256, 256], P('region', 'sector'), may hold values from -4 to 4
- right_env: bfloat16 [4, 8, 18, 256, 256], P('region', 'sector'), may hold values from -4 to 4
- diagonal: bfloat16 [4, 8, 256, 256], P('region', 'sector'), may hold values from -2 to 0
- left_coeff: float32 [18, 18], replicated, may hold values from -2 to 2
- right_coeff: float32 [18, 18], replicated, may hold values from -2 to 2
- mpo_mask: int32 [18, 18], replicated, may hold values 0 or 1
- sector_target: int32 [8, 18], P('sector'), may hold values from 0 to 7
- block_size: int32 [8], P('sector'), may hold values from 128 to 256, as said below
Outputs:
- bond: bfloat16 [4, 8, 256, 256], P('region', 'sector')
- energy: float32 [4], P('region')
Inputs may be any that keep to these rules, and one draw needn't show every extreme that they name: `block_size`: one sector block has all 256 rows live, and one has exactly 128.
All inputs are finite; a program needn't handle non-finite values.
Results may differ from a plain program's by a relative error of at most 0.017.
Values may be sent and summed in bfloat16 or wider, within the bound.
A program may use at most 64 MiB of HBM per device.

v0:
```python
import math

import jax
import jax.numpy as jnp
from jax import lax
from jax.sharding import PartitionSpec as P

ITERS = 2


step_size = 0.5


def shifted(value, axis, steps):
    count = lax.axis_size(axis)
    leading, last = (max(0, -steps), min(count, count - steps))
    return lax.ppermute(value, axis, [(source, source + steps) for source in range(leading, last)])


def carry_left(masked, env_blocks, mixing, rescale):
    left_half = jnp.einsum(
        "wij,jk->wik", env_blocks, masked, preferred_element_type=jnp.float32
    ).astype(jnp.bfloat16)
    left_terms = jnp.einsum("ji,wjk->wik", masked, left_half, preferred_element_type=jnp.float32)
    mixed = jnp.einsum("vw,wik->vik", mixing, left_terms, precision=lax.Precision.HIGHEST)
    return (rescale * mixed).astype(jnp.bfloat16)


def carry_right(masked, env_blocks, mixing, rescale):
    right_half = jnp.einsum(
        "wij,kj->wik", env_blocks, masked, preferred_element_type=jnp.float32
    ).astype(jnp.bfloat16)
    right_terms = jnp.einsum("ij,wjk->wik", masked, right_half, preferred_element_type=jnp.float32)
    mixed = jnp.einsum("vw,wik->vik", mixing, right_terms, precision=lax.Precision.HIGHEST)
    return (rescale * mixed).astype(jnp.bfloat16)


def local(
    psi, left_env, right_env, diagonal, left_coeff, right_coeff, mpo_mask, sector_target, block_size
):
    sectors = lax.axis_size("sector")
    block_width = psi.shape[-1]
    mpo_terms = left_env.shape[2]
    live_rows = jnp.arange(block_width, dtype=jnp.int32) < block_size[0]
    keep_mask = (live_rows[:, None] & live_rows[None, :]).astype(jnp.float32)
    masked = (psi[0, 0].astype(jnp.float32) * keep_mask).astype(jnp.bfloat16)
    wide = masked.astype(jnp.float32)
    start_norm = lax.psum(jnp.sum(wide * wide), "sector")
    rescale = sectors * block_width / start_norm
    pattern = mpo_mask.astype(jnp.float32)
    left_out = carry_left(masked, left_env[0, 0], left_coeff * pattern, rescale)
    right_out = carry_right(masked, right_env[0, 0], right_coeff * pattern, rescale)
    region_index = lax.axis_index("region")
    at_start = region_index == 0
    at_end = region_index == lax.axis_size("region") - 1
    from_left = shifted(left_out, "region", 1)
    from_right = shifted(right_out, "region", -1)
    left_used = jnp.where(at_start, left_env[0, 0], from_left)
    right_used = jnp.where(at_end, right_env[0, 0], from_right)
    routing = (sector_target[0][:, None] == jnp.arange(sectors, dtype=jnp.int32)[None, :]).astype(
        jnp.float32
    )
    inv_root = 1.0 / math.sqrt(mpo_terms)
    diag_here = diagonal[0, 0].astype(jnp.float32)
    total_cells = sectors * block_width * block_width
    vector = (wide * jnp.sqrt(total_cells / start_norm)).astype(jnp.bfloat16)
    energy = jnp.zeros((), jnp.float32)
    for step in range(ITERS):
        applied = jnp.einsum(
            "wij,jk->wik", left_used, vector, preferred_element_type=jnp.float32
        ).astype(jnp.bfloat16)
        product = jnp.einsum(
            "wik,wkl->wil", applied, right_used, preferred_element_type=jnp.float32
        )
        partials = (
            jnp.einsum("wt,wil->til", routing, product, precision=lax.Precision.HIGHEST) * inv_root
        )
        summed = lax.psum_scatter(
            partials.astype(jnp.bfloat16), "sector", scatter_dimension=0, tiled=True
        ).astype(jnp.float32)
        current = vector.astype(jnp.float32)
        applied_h = (summed[0] + diag_here * current) * keep_mask
        intersection, cross = lax.psum(
            (jnp.sum(current * current), jnp.sum(current * applied_h)), "sector"
        )
        energy = cross / intersection
        update = current - step_size * (applied_h - energy * current)
        norm_sq = lax.psum(jnp.sum(update * update), "sector")
        vector = (update * jnp.sqrt(total_cells / norm_sq)).astype(jnp.bfloat16)
    return (vector[None, None], jnp.reshape(energy, (1,)))


def solution(mesh):
    in_specs = (
        P("region", "sector", None, None),
        P("region", "sector", None, None, None),
        P("region", "sector", None, None, None),
        P("region", "sector", None, None),
        P(),
        P(),
        P(),
        P("sector", None),
        P("sector"),
    )
    out_specs = (P("region", "sector", None, None), P("region"))
    return jax.shard_map(local, mesh=mesh, in_specs=in_specs, out_specs=out_specs, check_vma=False)
```

profile of v0, /device:TPU:2, one launch (start us, length us, event | category | flops | bytes accessed | tf_op | source)
XLA Modules:
  0.0 356.3 jit_solution(6555994667109751597)
XLA Ops:
  9.5 22.3 %psum.49 = f32[]{:T(128)} all-reduce(f32[]{:T(128)} %fusion.44), channel_id=1, replica_groups=mesh['region'=4,'sector'=8] {'sector'}, use_global_device_ids=true, to_apply=%region_1.0 | all-reduce | flops 1 | bytes 8 | tf_op jit(solution)/shard_map/psum | solution.py:48
  31.8 5.3 %fusion.31 = f32[18,256,256]{1,2,0:T(8,128)} fusion(bf16[1,1,18,256,256]{4,3,2,1,0:T(8,128)(2,1)} %param.11, bf16[1,1,256,256]{3,2,1,0:T(8,128)(2,1)} %param.9, pred[256]{0:T(512)(128)(4,1)S(1)} %iota_compare_fusion.1), kind=kOutput, calls=%fused_computation.23 | convolution fusion | flops 1209663488 | bytes 7209216 | tf_op jit(solution)/shard_map/ij,wjk->wik/dot_general | solution.py:33
  37.1 6.3 %copy.21 = f32[18,256,256]{2,0,1:T(8,128)} copy(f32[18,256,256]{1,2,0:T(8,128)} %fusion.31) | data formatting | bytes 9437184 | tf_op jit(solution)/shard_map/ij,wjk->wik/transpose | solution.py:33
  44.2 7.4 %multiply_convert_fusion = bf16[18,256,256]{2,0,1:T(8,128)(2,1)S(1)} fusion(f32[]{:T(128)S(6)} %div.19, f32[18,256,256]{2,0,1:T(8,128)} %copy.21, f32[18,18]{1,0:T(8,128)S(1)} %copy-done.5, s32[18,18]{1,0:T(8,128)S(1)} %copy-done.4), kind=kOutput, calls=%fused_computation.4 | convolution fusion | flops 257163904 | bytes 7080484 | tf_op jit(solution)/shard_map/vw,wik->vik/dot_general | solution.py:34
  51.6 1.9 copy.22
  53.5 1.9 collective-permute-start.1
  55.5 3.8 %fusion.22 = f32[18,256,256]{1,2,0:T(8,128)} fusion(bf16[1,1,18,256,256]{4,3,2,1,0:T(8,128)(2,1)S(1)} %copy-done, bf16[1,1,256,256]{3,2,1,0:T(8,128)(2,1)S(1)} %copy-done.1, pred[256]{0:T(512)(128)(4,1)S(1)} %iota_compare_fusion.1), kind=kOutput, calls=%fused_computation.22 | convolution fusion | flops 1209663488 | bytes 7209216 | tf_op jit(solution)/shard_map/ji,wjk->wik/dot_general | solution.py:24
  59.3 6.3 %copy.19 = f32[18,256,256]{2,0,1:T(8,128)} copy(f32[18,256,256]{1,2,0:T(8,128)} %fusion.22) | data formatting | bytes 9437184 | tf_op jit(solution)/shard_map/ji,wjk->wik/transpose | solution.py:24
  65.6 7.4 %multiply_convert_fusion.1 = bf16[18,256,256]{2,0,1:T(8,128)(2,1)S(1)} fusion(f32[]{:T(128)S(6)} %div.19, f32[18,256,256]{2,0,1:T(8,128)} %copy.19, f32[18,18]{1,0:T(8,128)S(1)} %copy-done.6, s32[18,18]{1,0:T(8,128)S(1)} %copy-done.4), kind=kOutput, calls=%fused_computation.5 | convolution fusion | flops 257163904 | bytes 7080484 | tf_op jit(solution)/shard_map/vw,wik->vik/dot_general | solution.py:25
  73.0 2.0 copy.20
  75.0 4.0 %collective-permute-start = (bf16[18,256,256]{2,1,0:T(8,128)(2,1)}, bf16[18,256,256]{2,1,0:T(8,128)(2,1)}, u32[]{:S(2)}, u32[]{:S(2)}) collective-permute-start(bf16[18,256,256]{2,1,0:T(8,128)(2,1)} %copy.20), channel_id=1, source_target_pairs={{0,8},{8,16},{16,24},{1,9},{9,17},{17,25},{2,10},{10,18},{18,26},{... | collective-permute-start | bytes 7077896 | tf_op jit(solution)/shard_map/ppermute | solution.py:17
  79.8 2.3 collective-permute-done.1
  82.1 23.4 %collective-permute-done = bf16[18,256,256]{2,1,0:T(8,128)(2,1)} collective-permute-done((bf16[18,256,256]{2,1,0:T(8,128)(2,1)}, bf16[18,256,256]{2,1,0:T(8,128)(2,1)}, u32[]{:S(2)}, u32[]{:S(2)}) %collective-permute-start) | collective-permute-done | bytes 2359328 | tf_op jit(solution)/shard_map/ppermute | solution.py:17
  105.5 6.8 %fusion.15 = f32[18,256,256]{2,1,0:T(8,128)} fusion(bf16[18,256,256]{2,1,0:T(8,128)(2,1)} %collective-permute-done, bf16[1,1,18,256,256]{4,3,2,1,0:T(8,128)(2,1)S(1)} %copy-done, pred[]{:T(512)S(6)} %eq.25, bf16[18,256,256]{2,1,0:T(8,128)(2,1)} %collective-permute-done.1, bf16[1,1,18,256,256]{4,3,2,1,0:T(8,128)(2,1)} %param.11, pred[]{:T(512)S(6)} %eq.26, ...), kind=kOutput, calls=%fused_computation.19 | convolution fusion | flops 1211957248 | bytes 14287110 | tf_op jit(solution)/shard_map/wik,wkl->wil/dot_general | solution.py:72
  112.3 6.8 %multiply_convert_fusion.3 = bf16[8,256,256]{2,0,1:T(8,128)(2,1)S(1)} fusion(f32[18,256,256]{2,1,0:T(8,128)} %fusion.15, s32[18]{0:T(128)S(1)} %bitcast.169), kind=kOutput, calls=%fused_computation.27 | convolution fusion | flops 114294928 | bytes 5767240 | tf_op jit(solution)/shard_map/wt,wil->til/dot_general | solution.py:76
  120.4 60.8 %reduce-scatter.3.cloned.1.call-done = bf16[1,256,256]{2,1,0:T(8,128)(2,1)} async-done(((bf16[8,256,256]{2,1,0:T(8,128)(2,1)}), bf16[1,256,256]{2,1,0:T(8,128)(2,1)}) %reduce-scatter.3.cloned.1.call-update) | async-done | bytes 131088 | tf_op jit(solution)/shard_map/reduce_scatter | solution.py:78
  182.9 20.1 %all-reduce.1 = (f32[]{:T(128)}, f32[]{:T(128)}) all-reduce(f32[]{:T(128)} %get-tuple-element.3, f32[]{:T(128)} %get-tuple-element.2), channel_id=1, replica_groups=mesh['region'=4,'sector'=8] {'sector'}, use_global_device_ids=true, to_apply=%region_4.5 | all-reduce | flops 2 | bytes 16 | tf_op jit(solution)/shard_map/psum | solution.py:83
  206.1 18.0 %psum.52 = f32[]{:T(128)} all-reduce(f32[]{:T(128)} %multiply_reduce_fusion), channel_id=1, replica_groups=mesh['region'=4,'sector'=8] {'sector'}, use_global_device_ids=true, to_apply=%region_8.9 | all-reduce | flops 1 | bytes 8 | tf_op jit(solution)/shard_map/psum | solution.py:88
  225.9 6.7 %fusion.12 = f32[18,256,256]{2,1,0:T(8,128)} fusion(bf16[18,256,256]{2,1,0:T(8,128)(2,1)} %collective-permute-done, bf16[1,1,18,256,256]{4,3,2,1,0:T(8,128)(2,1)S(1)} %copy-done, pred[]{:T(512)S(6)} %eq.25, bf16[18,256,256]{2,1,0:T(8,128)(2,1)} %collective-permute-done.1, bf16[1,1,18,256,256]{4,3,2,1,0:T(8,128)(2,1)} %param.11, pred[]{:T(512)S(6)} %eq.26, ...), kind=kOutput, calls=%fused_computation.16 | convolution fusion | flops 1211498496 | bytes 14286850 | tf_op jit(solution)/shard_map/wik,wkl->wil/dot_general | solution.py:72
  232.6 6.8 %multiply_convert_fusion.2 = bf16[8,256,256]{2,0,1:T(8,128)(2,1)S(1)} fusion(f32[18,256,256]{2,1,0:T(8,128)} %fusion.12, s32[18]{0:T(128)S(1)} %bitcast.170), kind=kOutput, calls=%fused_computation.26 | convolution fusion | flops 114294928 | bytes 5767240 | tf_op jit(solution)/shard_map/wt,wil->til/dot_general | solution.py:76
  240.7 62.6 %reduce-scatter.5.cloned.1.call-done = bf16[1,256,256]{2,1,0:T(8,128)(2,1)} async-done(((bf16[8,256,256]{2,1,0:T(8,128)(2,1)}), bf16[1,256,256]{2,1,0:T(8,128)(2,1)}) %reduce-scatter.5.cloned.1.call-update) | async-done | bytes 131088 | tf_op jit(solution)/shard_map/reduce_scatter | solution.py:78
  305.0 20.0 %all-reduce = (f32[]{:T(128)}, f32[]{:T(128)}) all-reduce(f32[]{:T(128)} %get-tuple-element.5, f32[]{:T(128)} %get-tuple-element.4), channel_id=1, replica_groups=mesh['region'=4,'sector'=8] {'sector'}, use_global_device_ids=true, to_apply=%region_11.12 | all-reduce | flops 2 | bytes 16 | tf_op jit(solution)/shard_map/psum | solution.py:83
  328.0 17.7 %psum.55 = f32[]{:T(128)} all-reduce(f32[]{:T(128)} %fusion.69), channel_id=1, replica_groups=mesh['region'=4,'sector'=8] {'sector'}, use_global_device_ids=true, to_apply=%region_15.16 | all-reduce | flops 1 | bytes 8 | tf_op jit(solution)/shard_map/psum | solution.py:88
  346.5 1.8 fusion.57
  (29 shorter events, 12.1 us)
Async XLA Ops:
  7.2 174.0 %reduce-scatter.3.cloned.1.call-start = ((), (), s32[]{:S(2)}) async-start(), calls=%async_computation.2 | async-start | bytes 1179648 | tf_op jit(solution)/shard_map/reduce_scatter | solution.py:78
  37.1 7.0 %copy-start.4 = (s32[18,18]{1,0:T(8,128)S(1)}, s32[18,18]{1,0:T(8,128)}, u32[]{:S(2)}) copy-start(s32[18,18]{1,0:T(8,128)} %param.15) | copy-start | bytes 3892
  37.1 7.1 %copy-start.5 = (f32[18,18]{1,0:T(8,128)S(1)}, f32[18,18]{1,0:T(8,128)}, u32[]{:S(2)}) copy-start(f32[18,18]{1,0:T(8,128)} %param.14) | copy-start | bytes 3892
  51.6 3.8 %copy-start = (bf16[1,1,18,256,256]{4,3,2,1,0:T(8,128)(2,1)S(1)}, bf16[1,1,18,256,256]{4,3,2,1,0:T(8,128)(2,1)}, u32[]{:S(2)}) copy-start(bf16[1,1,18,256,256]{4,3,2,1,0:T(8,128)(2,1)} %param.10) | copy-start | bytes 7077892
  51.6 3.8 %copy-start.1 = (bf16[1,1,256,256]{3,2,1,0:T(8,128)(2,1)S(1)}, bf16[1,1,256,256]{3,2,1,0:T(8,128)(2,1)}, u32[]{:S(2)}) copy-start(bf16[1,1,256,256]{3,2,1,0:T(8,128)(2,1)} %param.9) | copy-start | bytes 393220
  53.5 28.6 %collective-permute-start.1 = (bf16[18,256,256]{2,1,0:T(8,128)(2,1)}, bf16[18,256,256]{2,1,0:T(8,128)(2,1)}, u32[]{:S(2)}, u32[]{:S(2)}) collective-permute-start(bf16[18,256,256]{2,1,0:T(8,128)(2,1)} %copy.22), channel_id=1, source_target_pairs={{8,0},{16,8},{24,16},{9,1},{17,9},{25,17},{10,2},{18,10},{26,18},{... | collective-permute-start | bytes 7077896 | tf_op jit(solution)/shard_map/ppermute | solution.py:17
  59.3 6.3 %copy-start.6 = (f32[18,18]{1,0:T(8,128)S(1)}, f32[18,18]{1,0:T(8,128)}, u32[]{:S(2)}) copy-start(f32[18,18]{1,0:T(8,128)} %param.13) | copy-start | bytes 3892
  75.0 30.5 %collective-permute-start = (bf16[18,256,256]{2,1,0:T(8,128)(2,1)}, bf16[18,256,256]{2,1,0:T(8,128)(2,1)}, u32[]{:S(2)}, u32[]{:S(2)}) collective-permute-start(bf16[18,256,256]{2,1,0:T(8,128)(2,1)} %copy.20), channel_id=1, source_target_pairs={{0,8},{8,16},{16,24},{1,9},{9,17},{17,25},{2,10},{10,18},{18,26},{... | collective-permute-start | bytes 7077896 | tf_op jit(solution)/shard_map/ppermute | solution.py:17
  79.8 32.5 %copy-start.7 = (s32[1,18]{1,0:T(1,128)S(1)}, s32[1,18]{1,0:T(1,128)}, u32[]{:S(2)}) copy-start(s32[1,18]{1,0:T(1,128)} %param.16) | copy-start | bytes 220
  119.1 62.0 %copy-start.2 = (bf16[1,1,256,256]{3,2,1,0:T(8,128)(2,1)S(1)}, bf16[1,1,256,256]{3,2,1,0:T(8,128)(2,1)}, u32[]{:S(2)}) copy-start(bf16[1,1,256,256]{3,2,1,0:T(8,128)(2,1)} %param.12) | copy-start | bytes 393220
  120.3 183.0 %reduce-scatter.5.cloned.1.call-start = ((), (), s32[]{:S(2)}) async-start(), calls=%async_computation.3 | async-start | bytes 1179648 | tf_op jit(solution)/shard_map/reduce_scatter | solution.py:78
  239.4 107.1 %copy-start.3 = (bf16[1,256,256]{2,1,0:T(8,128)(2,1)S(1)}, bf16[1,256,256]{2,1,0:T(8,128)(2,1)}, u32[]{:S(2)}) copy-start(bf16[1,256,256]{2,1,0:T(8,128)(2,1)} %reduce-scatter.3.cloned.1.call-done) | copy-start | bytes 393220
Sparse Core Ops, SparseCore 0:
  120.4 60.6 reduce-scatter.2
  240.8 62.4 reduce-scatter.4
where the time goes:
time: 359 us; the launch traced here: 356 us
  waiting for transfers between devices  149 us (42%)
  blocking collectives  98.1 us (27%)
  matrix products  51.1 us (14%)
  between operations  21.5 us (6%)
  local copies, waits for them, and re-layouts  19 us (5%)
  other arithmetic  11.4 us (3%)
  starting transfers between devices  6.02 us (2%)
    reduce_scatter x2, waiting for transfers between devices, local(): lax.psum_scatter(partials.astype(jnp.bfloat16), 'sector', scatter_dimensi...  123 us
    psum x2, blocking collectives, local(): lax.psum((jnp.sum(current * current), jnp.sum(current * applied_h)), 'sec...  40.1 us
    psum x2, blocking collectives, local(): norm_sq = lax.psum(jnp.sum(update * update), 'sector')  35.7 us
    ppermute x2, waiting for transfers between devices, shifted(): lax.ppermute(value, axis, [(source, source + steps) for source in range(l...  25.7 us
    psum x1, blocking collectives, local(): start_norm = lax.psum(jnp.sum(wide * wide), 'sector')  22.3 us
    dot_general x2, matrix products, local(): jnp.einsum('wt,wil->til', routing, product, precision=lax.Precision.HIGHEST)  13.7 us
    dot_general x2, matrix products, local(): jnp.einsum('wik,wkl->wil', applied, right_used, preferred_element_type=jn...  13.5 us
    dot_general x1, matrix products, carry_right(): jnp.einsum('vw,wik->vik', mixing, right_terms, precision=lax.Precision.HI...  7.41 us
  transfers between devices with their start and end apart: 4, of which 4 were waited for; matrix products, arithmetic and copies ran while one was open for 5% of the time, Pallas kernels for 0%

commit v1 on v0

v1 whole, which is shorter than its diff:
```python
import functools
import math

import jax
import jax.numpy as jnp
from jax import lax
from jax.experimental import pallas as pl
from jax.experimental.pallas import tpu as pltpu
from jax.sharding import PartitionSpec as P

ITERS = 2
STEP = 0.5
SLABS = 4
F32 = jnp.float32
BF16 = jnp.bfloat16
MESH = pl.DeviceIdType.MESH


def nn(a, b):
    return lax.dot_general(a, b, (((1,), (0,)), ((), ())), preferred_element_type=F32)


def nt(a, b):
    return lax.dot_general(a, b, (((1,), (1,)), ((), ())), preferred_element_type=F32)


def iota(shape, dim):
    return lax.broadcasted_iota(jnp.int32, shape, dim)


def total(x):
    return jnp.sum(jnp.sum(x, axis=0, keepdims=True), axis=1, keepdims=True)


def kernel(
    regions, ys, zs, width, terms,
    psi_ref, left_hbm, right_hbm, diag_ref, lc_ref, rc_ref, mask_ref, target_ref, size_ref,
    bond_ref, energy_ref,
    env, mixed, frame, out_slow, out_fast, slow, fast, vec, unit, route,
    term, part, y_in, zsum, z_in, result, scal,
    load_sem, slow_send, slow_recv, fast_sem, y_send, y_recv, z_send, z_recv, s_send, s_recv,
):
    sectors = ys * zs
    rows = width // SLABS
    cells = float(sectors * width * width)
    region = lax.axis_index("region")
    me = lax.axis_index("sector")
    my_y, my_z = lax.rem(me, ys), lax.div(me, ys)
    odd = lax.rem(region, 2)
    even = odd == 0
    fast_peer = region + 1 - 2 * odd
    slow_peer = region - 1 + 2 * odd
    inner = jnp.logical_and(slow_peer >= 0, slow_peer < regions)
    edge = jnp.logical_not(inner)

    barrier = pltpu.get_barrier_semaphore()
    for d in range(1, sectors):
        pl.semaphore_signal(
            barrier, inc=1, device_id={"sector": lax.rem(me + d, sectors)}, device_id_type=MESH
        )
    pl.semaphore_signal(barrier, inc=1, device_id={"region": fast_peer}, device_id_type=MESH)

    @pl.when(inner)
    def _():
        pl.semaphore_signal(barrier, inc=1, device_id={"region": slow_peer}, device_id_type=MESH)

    def load(source, slot):
        return pltpu.make_async_copy(source, env.at[slot], load_sem.at[slot])

    @pl.when(even)
    def _():
        load(right_hbm, 0).start()
        load(left_hbm, 1).start()

    @pl.when(jnp.logical_not(even))
    def _():
        load(left_hbm, 0).start()
        load(right_hbm, 1).start()

    size = size_ref[0]
    square = (width, width)
    keep = jnp.logical_and(iota(square, 0) < size, iota(square, 1) < size)
    unit[...] = jnp.where(iota(square, 0) == iota(square, 1), 1.0, 0.0).astype(BF16)
    wide = jnp.where(keep, psi_ref[...].astype(F32), 0.0)
    masked = wide.astype(BF16)
    turned = nt(unit[...], masked).astype(BF16)

    @pl.when(even)
    def _():
        frame[0] = masked
        frame[1] = turned

    @pl.when(jnp.logical_not(even))
    def _():
        frame[0] = turned
        frame[1] = masked

    lanes = iota((8, 128), 1)

    def scalar_copy(which, d):
        peer = lax.rem(me + d, sectors)
        return pltpu.make_async_remote_copy(
            src_ref=scal.at[which, me], dst_ref=scal.at[which, me],
            send_sem=s_send.at[which, d - 1], recv_sem=s_recv.at[which, d - 1],
            device_id={"sector": peer}, device_id_type=MESH,
        )

    def scalar_start(which, values):
        packed = jnp.zeros((8, 128), F32)
        for lane, value in enumerate(values):
            packed = jnp.where(lanes == lane, jnp.broadcast_to(value, (8, 128)), packed)
        scal[which, me] = packed
        for d in range(1, sectors):
            scalar_copy(which, d).start()

    def scalar_finish(which, count):
        for d in range(1, sectors):
            scalar_copy(which, d).wait_recv()
        added = jnp.sum(scal[which], axis=0)[0:1, :]
        return [
            jnp.sum(jnp.where(lanes[0:1] == lane, added, 0.0), axis=1, keepdims=True)
            for lane in range(count)
        ]

    pl.semaphore_wait(barrier, sectors + inner.astype(jnp.int32))

    scalar_start(0, [total(wide * wide)])

    tall = 8 * terms
    spread = jnp.where((iota((tall, terms), 0) >> 3) == iota((tall, terms), 1), 1.0, 0.0).astype(BF16)
    same = (iota((tall, tall), 0) & 7) == (iota((tall, tall), 1) & 7)
    pattern = mask_ref[...].astype(F32)

    def mixer(coeff):
        over = nn(spread, (coeff * pattern).astype(BF16)).astype(BF16)
        return jnp.where(same, nt(over, spread), 0.0).astype(BF16)

    left_c, right_c = lc_ref[...], rc_ref[...]
    parity = odd.astype(F32)
    mixers = [
        mixer(right_c + parity * (left_c - right_c)),
        mixer(left_c + parity * (right_c - left_c)),
    ]
    wanted = (sectors * 8, tall)
    aim = jnp.zeros(wanted, jnp.int32)
    for w in range(terms):
        aim = jnp.where((iota(wanted, 1) >> 3) == w, target_ref[0, w], aim)
    block = iota(wanted, 0) >> 3
    z_bits = zs.bit_length() - 1
    mine = (block & (zs - 1)) * ys + (block >> z_bits)
    hit = jnp.logical_and(aim == mine, (iota(wanted, 0) & 7) == (iota(wanted, 1) & 7))
    route[...] = jnp.where(hit, 1.0, 0.0).astype(BF16)

    def mix(slot):
        matrix = mixers[slot]

        def body(i, carry):
            start = pl.multiple_of(i * 16, 16)
            x = env[slot, :, pl.ds(start, 16), :].astype(F32)
            halves = []
            for h in range(2):
                piece = x[:, 8 * h : 8 * h + 8, :].reshape(tall, width).astype(BF16)
                halves.append(nn(matrix, piece).reshape(terms, 8, width))
            mixed[:, pl.ds(start, 16), :] = jnp.concatenate(halves, axis=1).astype(BF16)
            return carry

        lax.fori_loop(0, width // 16, body, 0)

    group = 3 if terms % 3 == 0 else (2 if terms % 2 == 0 else 1)

    def carry_env(slot, rescale, store):
        def body(i, carry):
            for j in range(group):
                v = i * group + j
                a = frame[slot]
                y = nn(a, mixed[v]).astype(BF16)
                first = jnp.where(even, a, y)
                second = jnp.where(even, y, a)
                store(v, (rescale * nt(first, second)).astype(BF16))
            return carry

        lax.fori_loop(0, terms // group, body, 0)

    def load_wait(slot):
        load(left_hbm, slot).wait()

    def slow_copy(k):
        return pltpu.make_async_remote_copy(
            src_ref=out_slow.at[k], dst_ref=slow.at[k],
            send_sem=slow_send.at[k], recv_sem=slow_recv.at[k],
            device_id={"region": slow_peer}, device_id_type=MESH,
        )

    fast_copy = pltpu.make_async_remote_copy(
        src_ref=out_fast, dst_ref=fast, send_sem=fast_sem.at[0], recv_sem=fast_sem.at[1],
        device_id={"region": fast_peer}, device_id_type=MESH,
    )

    load_wait(0)
    mix(0)
    (start_norm,) = scalar_finish(0, 1)
    rescale = sectors * width / start_norm

    def store_slow(v, value):
        for k in range(SLABS):
            out_slow[k, v] = value[k * rows : (k + 1) * rows]

    carry_env(0, rescale, store_slow)

    @pl.when(inner)
    def _():
        for k in range(min(2, SLABS)):
            slow_copy(k).start()

    load_wait(1)
    mix(1)

    def store_fast(v, value):
        out_fast[v] = value

    carry_env(1, rescale, store_fast)
    fast_copy.start()

    @pl.when(jnp.logical_and(edge, even))
    def _():
        def body(v, carry):
            for k in range(SLABS):
                slow[k, v] = env[1, v, k * rows : (k + 1) * rows, :]
            return carry

        lax.fori_loop(0, terms, body, 0)

    @pl.when(jnp.logical_and(edge, jnp.logical_not(even)))
    def _():
        def body(v, carry):
            value = nt(unit[...], env[1, v]).astype(BF16)
            for k in range(SLABS):
                slow[k, v] = value[k * rows : (k + 1) * rows]
            return carry

        lax.fori_loop(0, terms, body, 0)

    vec[0] = (frame[0].astype(F32) * jnp.sqrt(cells / start_norm)).astype(BF16)
    diag = diag_ref[...]
    diag_frame = jnp.where(even, diag, nt(unit[...], diag).astype(BF16))
    inv_root = 1.0 / math.sqrt(terms)

    def y_copy(it, k, d):
        peer_y = lax.rem(my_y + d, ys)
        return pltpu.make_async_remote_copy(
            src_ref=part.at[it, k, peer_y], dst_ref=y_in.at[it, k, d - 1],
            send_sem=y_send.at[it, k, d - 1], recv_sem=y_recv.at[it, k, d - 1],
            device_id={"sector": my_z * ys + peer_y}, device_id_type=MESH,
        )

    def z_copy(it, k, d):
        peer_z = lax.rem(my_z + d, zs)
        return pltpu.make_async_remote_copy(
            src_ref=zsum.at[it, k, peer_z], dst_ref=z_in.at[it, k, d - 1],
            send_sem=z_send.at[it, k, d - 1], recv_sem=z_recv.at[it, k, d - 1],
            device_id={"sector": peer_z * ys + my_y}, device_id_type=MESH,
        )

    def z_phase(it, k):
        for d in range(1, ys):
            y_copy(it, k, d).wait_recv()
        added = part[it, k, my_y].astype(F32)
        for d in range(1, ys):
            added = added + y_in[it, k, d - 1].astype(F32)
        zsum[it, k] = added.astype(BF16)
        for d in range(1, zs):
            z_copy(it, k, d).start()

    def apply(it):
        def body(k, carry):
            if it == 0:
                @pl.when(inner)
                def _():
                    slow_copy(k).wait_recv()

                @pl.when(jnp.logical_and(inner, k < SLABS - 2))
                def _():
                    slow_copy(k).wait_send()
                    slow_copy(k + 2).start()

            half = nn(slow[k].reshape(terms * rows, width), vec[it]).astype(BF16)
            for w in range(terms):
                term[w] = nn(half[w * rows : (w + 1) * rows], fast[w])
            matrix = route[...]
            for i in range(rows // 16):
                halves = []
                for h in range(2):
                    at = 16 * i + 8 * h
                    piece = term[:, at : at + 8, :].reshape(tall, width).astype(BF16)
                    halves.append((nn(matrix, piece) * inv_root).reshape(ys, zs, 8, width))
                part[it, k, :, :, 16 * i : 16 * i + 16, :] = jnp.concatenate(halves, axis=2).astype(BF16)
            for d in range(1, ys):
                y_copy(it, k, d).start()

            @pl.when(k >= 1)
            def _():
                z_phase(it, k - 1)

            return carry

        lax.fori_loop(0, SLABS, body, 0)
        z_phase(it, SLABS - 1)
        for k in range(SLABS):
            for d in range(1, zs):
                z_copy(it, k, d).wait_recv()
            added = zsum[it, k, my_z].astype(F32)
            for d in range(1, zs):
                added = added + z_in[it, k, d - 1].astype(F32)
            result[it, k * rows : (k + 1) * rows, :] = added
        source = vec[it].astype(F32)
        value = jnp.where(keep, result[it] + diag_frame.astype(F32) * source, 0.0)
        result[it] = value

    fast_copy.wait_recv()
    apply(0)
    first = result[0]
    vec[1] = first.astype(BF16)
    start = vec[0].astype(F32)
    scalar_start(1, [total(start * start), total(start * first), total(first * first)])
    apply(1)
    vv, vh, hh = scalar_finish(1, 3)
    energy = vh / vv
    near = 1.0 + STEP * energy
    scale = jnp.sqrt(cells / jnp.maximum(near * near * vv - 2.0 * STEP * near * vh + STEP * STEP * hh, vv))
    start = vec[0].astype(F32)
    first = result[0]
    x = scale * near * start - scale * STEP * first
    applied = scale * near * first - scale * STEP * result[1]
    y = applied - energy * x
    result[0] = x
    result[1] = y
    scalar_start(2, [total(x * x), total(x * y), total(y * y)])
    xx, xy, yy = scalar_finish(2, 3)
    gap = xy / xx
    norm = xx + STEP * STEP * jnp.maximum(yy - gap * xy, 0.0)
    grow = jnp.sqrt(cells / norm)
    bond = (grow * (result[0] - STEP * (result[1] - gap * result[0]))).astype(BF16)

    @pl.when(even)
    def _():
        bond_ref[...] = bond

    @pl.when(jnp.logical_not(even))
    def _():
        bond_ref[...] = nt(unit[...], bond).astype(BF16)

    energy_ref[...] = jnp.broadcast_to(energy + gap, (1, 128))

    for which in range(3):
        for d in range(1, sectors):
            scalar_copy(which, d).wait_send()
    fast_copy.wait_send()

    @pl.when(inner)
    def _():
        for k in range(max(0, SLABS - 2), SLABS):
            slow_copy(k).wait_send()

    for it in range(ITERS):
        for k in range(SLABS):
            for d in range(1, ys):
                y_copy(it, k, d).wait_send()
            for d in range(1, zs):
                z_copy(it, k, d).wait_send()


def local(regions, ys, zs, psi, left_env, right_env, diagonal, lc, rc, mask, target, size):
    width, terms = psi.shape[-1], left_env.shape[2]
    sectors, rows = ys * zs, width // SLABS
    envs = (terms, width, width)
    vmem = pl.BlockSpec(memory_space=pltpu.VMEM)
    smem = pl.BlockSpec(memory_space=pltpu.SMEM)
    hbm = pl.BlockSpec(memory_space=pl.ANY)
    dma = pltpu.SemaphoreType.DMA
    bond, energy = pl.pallas_call(
        functools.partial(kernel, regions, ys, zs, width, terms),
        out_shape=(
            jax.ShapeDtypeStruct((width, width), BF16),
            jax.ShapeDtypeStruct((1, 128), F32),
        ),
        in_specs=[vmem, hbm, hbm, vmem, vmem, vmem, vmem, smem, smem],
        out_specs=(vmem, vmem),
        scratch_shapes=[
            pltpu.VMEM((2,) + envs, BF16),
            pltpu.VMEM(envs, BF16),
            pltpu.VMEM((2, width, width), BF16),
            pltpu.VMEM((SLABS, terms, rows, width), BF16),
            pltpu.VMEM(envs, BF16),
            pltpu.VMEM((SLABS, terms, rows, width), BF16),
            pltpu.VMEM(envs, BF16),
            pltpu.VMEM((2, width, width), BF16),
            pltpu.VMEM((width, width), BF16),
            pltpu.VMEM((sectors * 8, terms * 8), BF16),
            pltpu.VMEM((terms, rows, width), F32),
            pltpu.VMEM((ITERS, SLABS, ys, zs, rows, width), BF16),
            pltpu.VMEM((ITERS, SLABS, max(ys - 1, 1), zs, rows, width), BF16),
            pltpu.VMEM((ITERS, SLABS, zs, rows, width), BF16),
            pltpu.VMEM((ITERS, SLABS, max(zs - 1, 1), rows, width), BF16),
            pltpu.VMEM((2, width, width), F32),
            pltpu.VMEM((3, sectors, 8, 128), F32),
            dma((2,)),
            dma((SLABS,)),
            dma((SLABS,)),
            dma((2,)),
            dma((ITERS, SLABS, max(ys - 1, 1))),
            dma((ITERS, SLABS, max(ys - 1, 1))),
            dma((ITERS, SLABS, max(zs - 1, 1))),
            dma((ITERS, SLABS, max(zs - 1, 1))),
            dma((3, sectors - 1)),
            dma((3, sectors - 1)),
        ],
        compiler_params=pltpu.CompilerParams(
            collective_id=0, has_side_effects=True, vmem_limit_bytes=56 * 2**20
        ),
    )(
        psi.reshape(width, width), left_env.reshape(envs), right_env.reshape(envs),
        diagonal.reshape(width, width), lc, rc, mask, target, size,
    )
    return bond.reshape(1, 1, width, width), energy[0, :1]


def solution(mesh):
    regions, sectors = mesh.shape["region"], mesh.shape["sector"]
    ys = 1
    while (2 * ys) * (2 * ys) * 2 <= sectors:
        ys *= 2
    in_specs = (
        P("region", "sector", None, None),
        P("region", "sector", None, None, None),
        P("region", "sector", None, None, None),
        P("region", "sector", None, None),
        P(),
        P(),
        P(),
        P("sector", None),
        P("sector"),
    )
    out_specs = (P("region", "sector", None, None), P("region"))
    body = functools.partial(local, regions, ys, sectors // ys)
    return jax.shard_map(body, mesh=mesh, in_specs=in_specs, out_specs=out_specs, check_vma=False)
```

time: 359 us -> 77.4 us (0.22)
  waiting for transfers between devices: 149 us -> 0 us
  blocking collectives: 98.1 us -> 0 us
  Pallas kernels: 0 us -> 72.6 us
  matrix products: 51.1 us -> 0 us
  between operations: 21.5 us -> 3.1 us
  local copies, waits for them, and re-layouts: 19 us -> 1.57 us
  other arithmetic: 11.4 us -> 0 us
  starting transfers between devices: 6.02 us -> 0 us
    reduce_scatter x2 -> x0, waiting for transfers between devices: 123 us -> none  [local(): lax.psum_scatter(partials.astype(jnp.bfloat16), 'sector', scatter_dimensi...]
    psum x5 -> x0, blocking collectives: 98.1 us -> none  [the longest x2 40.1 us: local(): lax.psum((jnp.sum(current * current), jnp.sum(current * applied_h)), 'sec...]
    pallas_call x0 -> x1, Pallas kernels: none -> 72.6 us  [local(): pl.pallas_call(functools.partial(kernel, regions, ys, zs, width, terms),...]
    dot_general x8 -> x0, matrix products: 51.1 us -> none  [the longest x2 13.7 us: local(): jnp.einsum('wt,wil->til', routing, product, precision=lax.Precision.HIGHEST)]
    ppermute x2 -> x0, waiting for transfers between devices: 25.7 us -> none  [shifted(): lax.ppermute(value, axis, [(source, source + steps) for source in range(l...]
    transpose x2 -> x0, local copies, waits for them, and re-layouts: 12.7 us -> none  [the longest x1 6.34 us: carry_right(): jnp.einsum('ij,wjk->wik', masked, right_half, preferred_element_type=jnp....]
    reduce_sum x5 -> x0, other arithmetic: 8.46 us -> none  [the longest x2 3.43 us: local(): norm_sq = lax.psum(jnp.sum(update * update), 'sector')]
    convert_element_type x4 -> x0, local copies, waits for them, and re-layouts: 6.24 us -> none  [the longest x2 2.37 us: local(): partials.astype(jnp.bfloat16)]
  transfers between devices with their start and end apart: 4 -> 0, of which waited for: 4 -> 0; matrix products, arithmetic and copies ran while one was open for 5% -> 0% of each run, Pallas kernels for 0% -> 0%
where the time goes in v1:
time: 77.4 us; the launch traced here: 77.3 us
  Pallas kernels  72.6 us (94%)
  between operations  3.1 us (4%)
  local copies, waits for them, and re-layouts  1.57 us (2%)
    pallas_call x1, Pallas kernels, local(): pl.pallas_call(functools.partial(kernel, regions, ys, zs, width, terms),...  72.6 us
    unnamed x1, local copies, waits for them, and re-layouts  1.57 us

profile of v1, /device:TPU:2, one launch (start us, length us, event | category | flops | bytes accessed | tf_op | source)
XLA Modules:
  0.0 77.3 jit_solution(10871887802275007443)
XLA Ops:
  1.3 72.6 %shard_map.104 = (bf16[256,256]{1,0:T(8,128)(2,1)}, f32[1,128]{1,0:T(1,128)}) custom-call(bf16[256,256]{1,0:T(8,128)(2,1)} %bitcast.9, bf16[18,256,256]{2,1,0:T(8,128)(2,1)} %bitcast.7, bf16[18,256,256]{2,1,0:T(8,128)(2,1)} %bitcast.8, bf16[256,256]{1,0:T(8,128)(2,1)} %bitcast.10, f32[18,18]{1,0:T(8,128)} %lc_ref.1, f32[18,18]{1,0:T(8,128)} %rc_ref.1, ...), custom_call_target="tpu_custom_call" | custom-call | tf_op jit(solution)/shard_map/pallas_call | solution.py:380
  73.9 1.6 %copy.14 = bf16[1,1,256,256]{3,2,1,0:T(8,128)(2,1)} copy(bf16[1,1,256,256]{3,2,1,0:T(8,128)(2,1)} %bitcast.11) | data formatting | bytes 262144

commit v2 on v1

--- a/solution.py
+++ b/solution.py
@@ -10,7 +10,8 @@
 
 ITERS = 2
 STEP = 0.5
-SLABS = 4
+SLABS = (8, 4)
+AHEAD = 2
 F32 = jnp.float32
 BF16 = jnp.bfloat16
 MESH = pl.DeviceIdType.MESH
@@ -37,11 +38,14 @@
     psi_ref, left_hbm, right_hbm, diag_ref, lc_ref, rc_ref, mask_ref, target_ref, size_ref,
     bond_ref, energy_ref,
     env, mixed, frame, out_slow, out_fast, slow, fast, vec, unit, route,
-    term, part, y_in, zsum, z_in, result, scal,
+    term, part0, part1, y_in0, y_in1, zsum0, zsum1, z_in0, z_in1, result, scal,
     load_sem, slow_send, slow_recv, fast_sem, y_send, y_recv, z_send, z_recv, s_send, s_recv,
 ):
     sectors = ys * zs
-    rows = width // SLABS
+    part, y_in = (part0, part1), (y_in0, y_in1)
+    zsum, z_in = (zsum0, zsum1), (z_in0, z_in1)
+    slabs = SLABS[0]
+    rows = width // slabs
     cells = float(sectors * width * width)
     region = lax.axis_index("region")
     me = lax.axis_index("sector")
@@ -155,18 +159,19 @@
         matrix = mixers[slot]
 
         def body(i, carry):
-            start = pl.multiple_of(i * 16, 16)
-            x = env[slot, :, pl.ds(start, 16), :].astype(F32)
-            halves = []
-            for h in range(2):
-                piece = x[:, 8 * h : 8 * h + 8, :].reshape(tall, width).astype(BF16)
-                halves.append(nn(matrix, piece).reshape(terms, 8, width))
-            mixed[:, pl.ds(start, 16), :] = jnp.concatenate(halves, axis=1).astype(BF16)
+            for j in range(4):
+                start = pl.multiple_of(i * 64 + j * 16, 16)
+                x = env[slot, :, pl.ds(start, 16), :].astype(F32)
+                halves = []
+                for h in range(2):
+                    piece = x[:, 8 * h : 8 * h + 8, :].reshape(tall, width).astype(BF16)
+                    halves.append(nn(matrix, piece).reshape(terms, 8, width))
+                mixed[:, pl.ds(start, 16), :] = jnp.concatenate(halves, axis=1).astype(BF16)
             return carry
 
-        lax.fori_loop(0, width // 16, body, 0)
-
-    group = 3 if terms % 3 == 0 else (2 if terms % 2 == 0 else 1)
+        lax.fori_loop(0, width // 64, body, 0)
+
+    group = max(g for g in range(1, 10) if terms % g == 0)
 
     def carry_env(slot, rescale, store):
         def body(i, carry):
@@ -202,14 +207,14 @@
     rescale = sectors * width / start_norm
 
     def store_slow(v, value):
-        for k in range(SLABS):
+        for k in range(slabs):
             out_slow[k, v] = value[k * rows : (k + 1) * rows]
 
     carry_env(0, rescale, store_slow)
 
     @pl.when(inner)
     def _():
-        for k in range(min(2, SLABS)):
+        for k in range(slabs - AHEAD):
             slow_copy(k).start()
 
     load_wait(1)
@@ -224,7 +229,7 @@
     @pl.when(jnp.logical_and(edge, even))
     def _():
         def body(v, carry):
-            for k in range(SLABS):
+            for k in range(slabs):
                 slow[k, v] = env[1, v, k * rows : (k + 1) * rows, :]
             return carry
 
@@ -234,7 +239,7 @@
     def _():
         def body(v, carry):
             value = nt(unit[...], env[1, v]).astype(BF16)
-            for k in range(SLABS):
+            for k in range(slabs):
                 slow[k, v] = value[k * rows : (k + 1) * rows]
             return carry
 
@@ -248,7 +253,7 @@
     def y_copy(it, k, d):
         peer_y = lax.rem(my_y + d, ys)
         return pltpu.make_async_remote_copy(
-            src_ref=part.at[it, k, peer_y], dst_ref=y_in.at[it, k, d - 1],
+            src_ref=part[it].at[k, peer_y], dst_ref=y_in[it].at[k, d - 1],
             send_sem=y_send.at[it, k, d - 1], recv_sem=y_recv.at[it, k, d - 1],
             device_id={"sector": my_z * ys + peer_y}, device_id_type=MESH,
         )
@@ -256,7 +261,7 @@
     def z_copy(it, k, d):
         peer_z = lax.rem(my_z + d, zs)
         return pltpu.make_async_remote_copy(
-            src_ref=zsum.at[it, k, peer_z], dst_ref=z_in.at[it, k, d - 1],
+            src_ref=zsum[it].at[k, peer_z], dst_ref=z_in[it].at[k, d - 1],
             send_sem=z_send.at[it, k, d - 1], recv_sem=z_recv.at[it, k, d - 1],
             device_id={"sector": peer_z * ys + my_y}, device_id_type=MESH,
         )
@@ -264,54 +269,66 @@
     def z_phase(it, k):
         for d in range(1, ys):
             y_copy(it, k, d).wait_recv()
-        added = part[it, k, my_y].astype(F32)
+        added = part[it][k, my_y].astype(F32)
         for d in range(1, ys):
-            added = added + y_in[it, k, d - 1].astype(F32)
-        zsum[it, k] = added.astype(BF16)
+            added = added + y_in[it][k, d - 1].astype(F32)
+        zsum[it][k] = added.astype(BF16)
         for d in range(1, zs):
             z_copy(it, k, d).start()
 
     def apply(it):
+        merge = slabs // SLABS[it]
+        tile = merge * rows
+
+        def z_before(k):
+            @pl.when(k >= 1)
+            def _():
+                z_phase(it, k - 1)
+
         def body(k, carry):
             if it == 0:
+                z_before(k)
+
                 @pl.when(inner)
                 def _():
                     slow_copy(k).wait_recv()
 
-                @pl.when(jnp.logical_and(inner, k < SLABS - 2))
+                @pl.when(jnp.logical_and(inner, k < AHEAD))
                 def _():
                     slow_copy(k).wait_send()
-                    slow_copy(k + 2).start()
-
-            half = nn(slow[k].reshape(terms * rows, width), vec[it]).astype(BF16)
+                    slow_copy(k + slabs - AHEAD).start()
+
+            left = slow[pl.ds(k * merge, merge)].reshape(merge * terms * rows, width)
+            half = nn(left, vec[it]).astype(BF16)
             for w in range(terms):
-                term[w] = nn(half[w * rows : (w + 1) * rows], fast[w])
+                pieces = [
+                    half[(j * terms + w) * rows : (j * terms + w + 1) * rows] for j in range(merge)
+                ]
+                term[w, 0:tile, :] = nn(jnp.concatenate(pieces, axis=0), fast[w])
             matrix = route[...]
-            for i in range(rows // 16):
+            for i in range(tile // 16):
                 halves = []
                 for h in range(2):
                     at = 16 * i + 8 * h
                     piece = term[:, at : at + 8, :].reshape(tall, width).astype(BF16)
                     halves.append((nn(matrix, piece) * inv_root).reshape(ys, zs, 8, width))
-                part[it, k, :, :, 16 * i : 16 * i + 16, :] = jnp.concatenate(halves, axis=2).astype(BF16)
+                both = jnp.concatenate(halves, axis=2).astype(BF16)
+                part[it][k, :, :, 16 * i : 16 * i + 16, :] = both
             for d in range(1, ys):
                 y_copy(it, k, d).start()
-
-            @pl.when(k >= 1)
-            def _():
-                z_phase(it, k - 1)
-
+            if it > 0:
+                z_before(k)
             return carry
 
-        lax.fori_loop(0, SLABS, body, 0)
-        z_phase(it, SLABS - 1)
-        for k in range(SLABS):
+        lax.fori_loop(0, SLABS[it], body, 0)
+        z_phase(it, SLABS[it] - 1)
+        for k in range(SLABS[it]):
             for d in range(1, zs):
                 z_copy(it, k, d).wait_recv()
-            added = zsum[it, k, my_z].astype(F32)
+            added = zsum[it][k, my_z].astype(F32)
             for d in range(1, zs):
-                added = added + z_in[it, k, d - 1].astype(F32)
-            result[it, k * rows : (k + 1) * rows, :] = added
+                added = added + z_in[it][k, d - 1].astype(F32)
+            result[it, k * tile : (k + 1) * tile, :] = added
         source = vec[it].astype(F32)
         value = jnp.where(keep, result[it] + diag_frame.astype(F32) * source, 0.0)
         result[it] = value
@@ -358,11 +375,11 @@
 
     @pl.when(inner)
     def _():
-        for k in range(max(0, SLABS - 2), SLABS):
+        for k in range(AHEAD, slabs):
             slow_copy(k).wait_send()
 
     for it in range(ITERS):
-        for k in range(SLABS):
+        for k in range(SLABS[it]):
             for d in range(1, ys):
                 y_copy(it, k, d).wait_send()
             for d in range(1, zs):
@@ -371,7 +388,9 @@
 
 def local(regions, ys, zs, psi, left_env, right_env, diagonal, lc, rc, mask, target, size):
     width, terms = psi.shape[-1], left_env.shape[2]
-    sectors, rows = ys * zs, width // SLABS
+    sectors, slabs = ys * zs, SLABS[0]
+    rows, tiles = width // slabs, [width // n for n in SLABS]
+    y_peers, z_peers = max(ys - 1, 1), max(zs - 1, 1)
     envs = (terms, width, width)
     vmem = pl.BlockSpec(memory_space=pltpu.VMEM)
     smem = pl.BlockSpec(memory_space=pltpu.SMEM)
@@ -389,28 +408,28 @@
             pltpu.VMEM((2,) + envs, BF16),
             pltpu.VMEM(envs, BF16),
             pltpu.VMEM((2, width, width), BF16),
-            pltpu.VMEM((SLABS, terms, rows, width), BF16),
+            pltpu.VMEM((slabs, terms, rows, width), BF16),
             pltpu.VMEM(envs, BF16),
-            pltpu.VMEM((SLABS, terms, rows, width), BF16),
+            pltpu.VMEM((slabs, terms, rows, width), BF16),
             pltpu.VMEM(envs, BF16),
             pltpu.VMEM((2, width, width), BF16),
             pltpu.VMEM((width, width), BF16),
             pltpu.VMEM((sectors * 8, terms * 8), BF16),
-            pltpu.VMEM((terms, rows, width), F32),
-            pltpu.VMEM((ITERS, SLABS, ys, zs, rows, width), BF16),
-            pltpu.VMEM((ITERS, SLABS, max(ys - 1, 1), zs, rows, width), BF16),
-            pltpu.VMEM((ITERS, SLABS, zs, rows, width), BF16),
-            pltpu.VMEM((ITERS, SLABS, max(zs - 1, 1), rows, width), BF16),
+            pltpu.VMEM((terms, max(tiles), width), F32),
+            *[pltpu.VMEM((n, ys, zs, width // n, width), BF16) for n in SLABS],
+            *[pltpu.VMEM((n, y_peers, zs, width // n, width), BF16) for n in SLABS],
+            *[pltpu.VMEM((n, zs, width // n, width), BF16) for n in SLABS],
+            *[pltpu.VMEM((n, z_peers, width // n, width), BF16) for n in SLABS],
             pltpu.VMEM((2, width, width), F32),
             pltpu.VMEM((3, sectors, 8, 128), F32),
             dma((2,)),
-            dma((SLABS,)),
-            dma((SLABS,)),
+            dma((slabs,)),
+            dma((slabs,)),
             dma((2,)),
-            dma((ITERS, SLABS, max(ys - 1, 1))),
-            dma((ITERS, SLABS, max(ys - 1, 1))),
-            dma((ITERS, SLABS, max(zs - 1, 1))),
-            dma((ITERS, SLABS, max(zs - 1, 1))),
+            dma((ITERS, slabs, y_peers)),
+            dma((ITERS, slabs, y_peers)),
+            dma((ITERS, slabs, z_peers)),
+            dma((ITERS, slabs, z_peers)),
             dma((3, sectors - 1)),
             dma((3, sectors - 1)),
         ],

time: 77.4 us -> 86.6 us (1.12); the launches traced: 77.3 us -> 85.5 us
  Pallas kernels: 72.6 us -> 80.8 us
    pallas_call x1, Pallas kernels: 72.6 us -> 80.8 us  [local(): pl.pallas_call(functools.partial(kernel, regions, ys, zs, width, terms),...]
where the time goes in v2:
time: 86.6 us; the launch traced here: 85.5 us
  Pallas kernels  80.8 us (93%)
  between operations  3.1 us (4%)
  local copies, waits for them, and re-layouts  1.57 us (2%)
    pallas_call x1, Pallas kernels, local(): pl.pallas_call(functools.partial(kernel, regions, ys, zs, width, terms),...  80.8 us

profile of v2, /device:TPU:2, one launch (start us, length us, event | category | flops | bytes accessed | tf_op | source)
XLA Modules:
  0.0 85.5 jit_solution(7007117022328789145)
XLA Ops:
  1.3 80.8 %shard_map.104 = (bf16[256,256]{1,0:T(8,128)(2,1)}, f32[1,128]{1,0:T(1,128)}) custom-call(bf16[256,256]{1,0:T(8,128)(2,1)} %bitcast.9, bf16[18,256,256]{2,1,0:T(8,128)(2,1)} %bitcast.7, bf16[18,256,256]{2,1,0:T(8,128)(2,1)} %bitcast.8, bf16[256,256]{1,0:T(8,128)(2,1)} %bitcast.10, f32[18,18]{1,0:T(8,128)} %lc_ref.1, f32[18,18]{1,0:T(8,128)} %rc_ref.1, ...), custom_call_target="tpu_custom_call" | custom-call | tf_op jit(solution)/shard_map/pallas_call | solution.py:399
  82.1 1.6 %copy.14 = bf16[1,1,256,256]{3,2,1,0:T(8,128)(2,1)} copy(bf16[1,1,256,256]{3,2,1,0:T(8,128)(2,1)} %bitcast.11) | data formatting | bytes 262144

commit v3 on v2

--- a/solution.py
+++ b/solution.py
@@ -10,8 +10,9 @@
 
 ITERS = 2
 STEP = 0.5
-SLABS = (8, 4)
-AHEAD = 2
+SLABS = (4, 4)
+LAGS = (1, 2)
+AHEAD = 1
 F32 = jnp.float32
 BF16 = jnp.bfloat16
 MESH = pl.DeviceIdType.MESH
@@ -214,7 +215,7 @@
 
     @pl.when(inner)
     def _():
-        for k in range(slabs - AHEAD):
+        for k in range(AHEAD):
             slow_copy(k).start()
 
     load_wait(1)
@@ -225,6 +226,11 @@
 
     carry_env(1, rescale, store_fast)
     fast_copy.start()
+
+    @pl.when(inner)
+    def _():
+        for k in range(AHEAD, slabs):
+            slow_copy(k).start()
 
     @pl.when(jnp.logical_and(edge, even))
     def _():
@@ -280,23 +286,13 @@
         merge = slabs // SLABS[it]
         tile = merge * rows
 
-        def z_before(k):
-            @pl.when(k >= 1)
-            def _():
-                z_phase(it, k - 1)
+        lag = LAGS[it]
 
         def body(k, carry):
             if it == 0:
-                z_before(k)
-
                 @pl.when(inner)
                 def _():
                     slow_copy(k).wait_recv()
-
-                @pl.when(jnp.logical_and(inner, k < AHEAD))
-                def _():
-                    slow_copy(k).wait_send()
-                    slow_copy(k + slabs - AHEAD).start()
 
             left = slow[pl.ds(k * merge, merge)].reshape(merge * terms * rows, width)
             half = nn(left, vec[it]).astype(BF16)
@@ -316,12 +312,16 @@
                 part[it][k, :, :, 16 * i : 16 * i + 16, :] = both
             for d in range(1, ys):
                 y_copy(it, k, d).start()
-            if it > 0:
-                z_before(k)
+
+            @pl.when(k >= lag)
+            def _():
+                z_phase(it, k - lag)
+
             return carry
 
         lax.fori_loop(0, SLABS[it], body, 0)
-        z_phase(it, SLABS[it] - 1)
+        for k in range(SLABS[it] - lag, SLABS[it]):
+            z_phase(it, k)
         for k in range(SLABS[it]):
             for d in range(1, zs):
                 z_copy(it, k, d).wait_recv()
@@ -375,7 +375,7 @@
 
     @pl.when(inner)
     def _():
-        for k in range(AHEAD, slabs):
+        for k in range(slabs):
             slow_copy(k).wait_send()
 
     for it in range(ITERS):

time: 86.6 us -> 74.2 us (0.86); the launches traced: 85.5 us -> 74 us
  Pallas kernels: 80.8 us -> 69.4 us
    pallas_call x1, Pallas kernels: 80.8 us -> 69.4 us  [local(): pl.pallas_call(functools.partial(kernel, regions, ys, zs, width, terms),...]
where the time goes in v3:
time: 74.2 us; the launch traced here: 74 us
  Pallas kernels  69.4 us (94%)
  between operations  3.1 us (4%)
  local copies, waits for them, and re-layouts  1.57 us (2%)
    pallas_call x1, Pallas kernels, local(): pl.pallas_call(functools.partial(kernel, regions, ys, zs, width, terms),...  69.4 us
    unnamed x1, local copies, waits for them, and re-layouts  1.57 us

profile of v3, /device:TPU:2, one launch (start us, length us, event | category | flops | bytes accessed | tf_op | source)
XLA Modules:
  0.0 74.0 jit_solution(6494613970239478314)
XLA Ops:
  1.3 69.4 %shard_map.104 = (bf16[256,256]{1,0:T(8,128)(2,1)}, f32[1,128]{1,0:T(1,128)}) custom-call(bf16[256,256]{1,0:T(8,128)(2,1)} %bitcast.9, bf16[18,256,256]{2,1,0:T(8,128)(2,1)} %bitcast.7, bf16[18,256,256]{2,1,0:T(8,128)(2,1)} %bitcast.8, bf16[256,256]{1,0:T(8,128)(2,1)} %bitcast.10, f32[18,18]{1,0:T(8,128)} %lc_ref.1, f32[18,18]{1,0:T(8,128)} %rc_ref.1, ...), custom_call_target="tpu_custom_call" | custom-call | tf_op jit(solution)/shard_map/pallas_call | solution.py:399
  70.7 1.6 %copy.14 = bf16[1,1,256,256]{3,2,1,0:T(8,128)(2,1)} copy(bf16[1,1,256,256]{3,2,1,0:T(8,128)(2,1)} %bitcast.11) | data formatting | bytes 262144

commit v4 on v3

--- a/solution.py
+++ b/solution.py
@@ -37,10 +37,10 @@
 def kernel(
     regions, ys, zs, width, terms,
     psi_ref, left_hbm, right_hbm, diag_ref, lc_ref, rc_ref, mask_ref, target_ref, size_ref,
-    bond_ref, energy_ref,
+    bond_ref, energy_ref, hbm_out, hbm_in,
     env, mixed, frame, out_slow, out_fast, slow, fast, vec, unit, route,
     term, part0, part1, y_in0, y_in1, zsum0, zsum1, z_in0, z_in1, result, scal,
-    load_sem, slow_send, slow_recv, fast_sem, y_send, y_recv, z_send, z_recv, s_send, s_recv,
+    load_sem, stage_sem, slow_send, slow_recv, fast_sem, y_send, y_recv, z_send, z_recv, s_send, s_recv,
 ):
     sectors = ys * zs
     part, y_in = (part0, part1), (y_in0, y_in1)
@@ -192,10 +192,16 @@
 
     def slow_copy(k):
         return pltpu.make_async_remote_copy(
-            src_ref=out_slow.at[k], dst_ref=slow.at[k],
+            src_ref=hbm_out.at[k], dst_ref=hbm_in.at[k],
             send_sem=slow_send.at[k], recv_sem=slow_recv.at[k],
             device_id={"region": slow_peer}, device_id_type=MESH,
         )
+
+    def stage_out(k):
+        return pltpu.make_async_copy(out_slow.at[k], hbm_out.at[k], stage_sem.at[0, k])
+
+    def stage_in(k):
+        return pltpu.make_async_copy(hbm_in.at[k], slow.at[k], stage_sem.at[1, k])
 
     fast_copy = pltpu.make_async_remote_copy(
         src_ref=out_fast, dst_ref=fast, send_sem=fast_sem.at[0], recv_sem=fast_sem.at[1],
@@ -215,7 +221,10 @@
 
     @pl.when(inner)
     def _():
+        for k in range(slabs):
+            stage_out(k).start()
         for k in range(AHEAD):
+            stage_out(k).wait()
             slow_copy(k).start()
 
     load_wait(1)
@@ -230,6 +239,7 @@
     @pl.when(inner)
     def _():
         for k in range(AHEAD, slabs):
+            stage_out(k).wait()
             slow_copy(k).start()
 
     @pl.when(jnp.logical_and(edge, even))
@@ -293,20 +303,22 @@
                 @pl.when(inner)
                 def _():
                     slow_copy(k).wait_recv()
-
-            left = slow[pl.ds(k * merge, merge)].reshape(merge * terms * rows, width)
-            half = nn(left, vec[it]).astype(BF16)
-            for w in range(terms):
-                pieces = [
-                    half[(j * terms + w) * rows : (j * terms + w + 1) * rows] for j in range(merge)
-                ]
-                term[w, 0:tile, :] = nn(jnp.concatenate(pieces, axis=0), fast[w])
+                    stage_in(k).start()
+                    stage_in(k).wait()
+
+            if it == 0:
+                half = nn(slow[k].reshape(terms * rows, width), vec[it]).astype(BF16)
+                for w in range(terms):
+                    term[w, 0:rows, :] = nn(half[w * rows : (w + 1) * rows], fast[w])
+                base = 0
+            else:
+                base = pl.multiple_of(k * tile, tile)
             matrix = route[...]
             for i in range(tile // 16):
                 halves = []
                 for h in range(2):
                     at = 16 * i + 8 * h
-                    piece = term[:, at : at + 8, :].reshape(tall, width).astype(BF16)
+                    piece = term[:, pl.ds(base + at, 8), :].reshape(tall, width).astype(BF16)
                     halves.append((nn(matrix, piece) * inv_root).reshape(ys, zs, 8, width))
                 both = jnp.concatenate(halves, axis=2).astype(BF16)
                 part[it][k, :, :, 16 * i : 16 * i + 16, :] = both
@@ -319,6 +331,12 @@
 
             return carry
 
+        if it > 0:
+            for k in range(slabs):
+                half = nn(slow[k].reshape(terms * rows, width), vec[it]).astype(BF16)
+                mixed[:, k * rows : (k + 1) * rows, :] = half.reshape(terms, rows, width)
+            for w in range(terms):
+                term[w] = nn(mixed[w], fast[w])
         lax.fori_loop(0, SLABS[it], body, 0)
         for k in range(SLABS[it] - lag, SLABS[it]):
             z_phase(it, k)
@@ -389,21 +407,23 @@
 def local(regions, ys, zs, psi, left_env, right_env, diagonal, lc, rc, mask, target, size):
     width, terms = psi.shape[-1], left_env.shape[2]
     sectors, slabs = ys * zs, SLABS[0]
-    rows, tiles = width // slabs, [width // n for n in SLABS]
+    rows = width // slabs
     y_peers, z_peers = max(ys - 1, 1), max(zs - 1, 1)
     envs = (terms, width, width)
     vmem = pl.BlockSpec(memory_space=pltpu.VMEM)
     smem = pl.BlockSpec(memory_space=pltpu.SMEM)
     hbm = pl.BlockSpec(memory_space=pl.ANY)
     dma = pltpu.SemaphoreType.DMA
-    bond, energy = pl.pallas_call(
+    bond, energy, _, _ = pl.pallas_call(
         functools.partial(kernel, regions, ys, zs, width, terms),
         out_shape=(
             jax.ShapeDtypeStruct((width, width), BF16),
             jax.ShapeDtypeStruct((1, 128), F32),
+            jax.ShapeDtypeStruct((slabs, terms, rows, width), BF16),
+            jax.ShapeDtypeStruct((slabs, terms, rows, width), BF16),
         ),
         in_specs=[vmem, hbm, hbm, vmem, vmem, vmem, vmem, smem, smem],
-        out_specs=(vmem, vmem),
+        out_specs=(vmem, vmem, hbm, hbm),
         scratch_shapes=[
             pltpu.VMEM((2,) + envs, BF16),
             pltpu.VMEM(envs, BF16),
@@ -415,7 +435,7 @@
             pltpu.VMEM((2, width, width), BF16),
             pltpu.VMEM((width, width), BF16),
             pltpu.VMEM((sectors * 8, terms * 8), BF16),
-            pltpu.VMEM((terms, max(tiles), width), F32),
+            pltpu.VMEM((terms, width, width), F32),
             *[pltpu.VMEM((n, ys, zs, width // n, width), BF16) for n in SLABS],
             *[pltpu.VMEM((n, y_peers, zs, width // n, width), BF16) for n in SLABS],
             *[pltpu.VMEM((n, zs, width // n, width), BF16) for n in SLABS],
@@ -423,6 +443,7 @@
             pltpu.VMEM((2, width, width), F32),
             pltpu.VMEM((3, sectors, 8, 128), F32),
             dma((2,)),
+            dma((2, slabs)),
             dma((slabs,)),
             dma((slabs,)),
             dma((2,)),

time: 74.2 us -> 76.6 us (1.032)
  Pallas kernels: 69.4 us -> 71.6 us
    pallas_call x1, Pallas kernels: 69.4 us -> 71.6 us  [local(): pl.pallas_call(functools.partial(kernel, regions, ys, zs, width, terms),...]
where the time goes in v4:
time: 76.6 us; the launch traced here: 76.3 us
  Pallas kernels  71.6 us (93%)
  between operations  3.11 us (4%)
  local copies, waits for them, and re-layouts  1.57 us (2%)
    pallas_call x1, Pallas kernels, local(): pl.pallas_call(functools.partial(kernel, regions, ys, zs, width, terms),...  71.6 us
    unnamed x1, local copies, waits for them, and re-layouts  1.57 us

profile of v4, /device:TPU:2, one launch (start us, length us, event | category | flops | bytes accessed | tf_op | source)
XLA Modules:
  0.0 76.3 jit_solution(18176157679933206213)
XLA Ops:
  1.3 71.6 %shard_map.104 = (bf16[256,256]{1,0:T(8,128)(2,1)}, f32[1,128]{1,0:T(1,128)}, bf16[4,18,64,256]{3,2,1,0:T(8,128)(2,1)}, bf16[4,18,64,256]{3,2,1,0:T(8,128)(2,1)}) custom-call(bf16[256,256]{1,0:T(8,128)(2,1)} %bitcast.9, bf16[18,256,256]{2,1,0:T(8,128)(2,1)} %bitcast.7, bf16[18,256,256]{2,1,0:T(8,128)(2,1)} %bitcast.8, bf16[256,256]{1,0:T(8,128)(2,1)} %bitcast.10, ...), custom_call_target="tpu_custom_call" | custom-call | tf_op jit(solution)/shard_map/pallas_call | solution.py:417
  72.9 1.6 %copy.14 = bf16[1,1,256,256]{3,2,1,0:T(8,128)(2,1)} copy(bf16[1,1,256,256]{3,2,1,0:T(8,128)(2,1)} %bitcast.11) | data formatting | bytes 262144

commit v5 on v3

--- a/solution.py
+++ b/solution.py
@@ -12,7 +12,6 @@
 STEP = 0.5
 SLABS = (4, 4)
 LAGS = (1, 2)
-AHEAD = 1
 F32 = jnp.float32
 BF16 = jnp.bfloat16
 MESH = pl.DeviceIdType.MESH
@@ -38,9 +37,9 @@
     regions, ys, zs, width, terms,
     psi_ref, left_hbm, right_hbm, diag_ref, lc_ref, rc_ref, mask_ref, target_ref, size_ref,
     bond_ref, energy_ref,
-    env, mixed, frame, out_slow, out_fast, slow, fast, vec, unit, route,
+    env, mixed, frame, peer_frame, raw, norms, out_slow, slow, fast, vec, unit, route,
     term, part0, part1, y_in0, y_in1, zsum0, zsum1, z_in0, z_in1, result, scal,
-    load_sem, slow_send, slow_recv, fast_sem, y_send, y_recv, z_send, z_recv, s_send, s_recv,
+    load_sem, slow_send, slow_recv, pair_send, pair_recv, y_send, y_recv, z_send, z_recv, s_send, s_recv,
 ):
     sectors = ys * zs
     part, y_in = (part0, part1), (y_in0, y_in1)
@@ -75,12 +74,10 @@
     @pl.when(even)
     def _():
         load(right_hbm, 0).start()
-        load(left_hbm, 1).start()
 
     @pl.when(jnp.logical_not(even))
     def _():
         load(left_hbm, 0).start()
-        load(right_hbm, 1).start()
 
     size = size_ref[0]
     square = (width, width)
@@ -131,6 +128,32 @@
 
     scalar_start(0, [total(wide * wide)])
 
+    def pair_copy(which, source, target):
+        return pltpu.make_async_remote_copy(
+            src_ref=source, dst_ref=target,
+            send_sem=pair_send.at[which], recv_sem=pair_recv.at[which],
+            device_id={"region": fast_peer}, device_id_type=MESH,
+        )
+
+    pair_copy(0, frame.at[1], peer_frame).start()
+
+    @pl.when(even)
+    def _():
+        pair_copy(1, left_hbm, raw).start()
+
+        @pl.when(edge)
+        def _():
+            load(left_hbm, 1).start()
+
+    @pl.when(jnp.logical_not(even))
+    def _():
+        pair_copy(1, right_hbm, raw).start()
+
+        @pl.when(edge)
+        def _():
+            load(right_hbm, 1).start()
+
+
     tall = 8 * terms
     spread = jnp.where((iota((tall, terms), 0) >> 3) == iota((tall, terms), 1), 1.0, 0.0).astype(BF16)
     same = (iota((tall, tall), 0) & 7) == (iota((tall, tall), 1) & 7)
@@ -142,10 +165,7 @@
 
     left_c, right_c = lc_ref[...], rc_ref[...]
     parity = odd.astype(F32)
-    mixers = [
-        mixer(right_c + parity * (left_c - right_c)),
-        mixer(left_c + parity * (right_c - left_c)),
-    ]
+    matrix_mix = mixer(right_c + parity * (left_c - right_c))
     wanted = (sectors * 8, tall)
     aim = jnp.zeros(wanted, jnp.int32)
     for w in range(terms):
@@ -156,17 +176,15 @@
     hit = jnp.logical_and(aim == mine, (iota(wanted, 0) & 7) == (iota(wanted, 1) & 7))
     route[...] = jnp.where(hit, 1.0, 0.0).astype(BF16)
 
-    def mix(slot):
-        matrix = mixers[slot]
-
+    def mix(source):
         def body(i, carry):
             for j in range(4):
                 start = pl.multiple_of(i * 64 + j * 16, 16)
-                x = env[slot, :, pl.ds(start, 16), :].astype(F32)
+                x = source[:, pl.ds(start, 16), :].astype(F32)
                 halves = []
                 for h in range(2):
                     piece = x[:, 8 * h : 8 * h + 8, :].reshape(tall, width).astype(BF16)
-                    halves.append(nn(matrix, piece).reshape(terms, 8, width))
+                    halves.append(nn(matrix_mix, piece).reshape(terms, 8, width))
                 mixed[:, pl.ds(start, 16), :] = jnp.concatenate(halves, axis=1).astype(BF16)
             return carry
 
@@ -174,14 +192,14 @@
 
     group = max(g for g in range(1, 10) if terms % g == 0)
 
-    def carry_env(slot, rescale, store):
+    def carry_env(factor, ahead, rescale, store):
         def body(i, carry):
             for j in range(group):
                 v = i * group + j
-                a = frame[slot]
+                a = factor[...]
                 y = nn(a, mixed[v]).astype(BF16)
-                first = jnp.where(even, a, y)
-                second = jnp.where(even, y, a)
+                first = jnp.where(ahead, a, y)
+                second = jnp.where(ahead, y, a)
                 store(v, (rescale * nt(first, second)).astype(BF16))
             return carry
 
@@ -197,13 +215,8 @@
             device_id={"region": slow_peer}, device_id_type=MESH,
         )
 
-    fast_copy = pltpu.make_async_remote_copy(
-        src_ref=out_fast, dst_ref=fast, send_sem=fast_sem.at[0], recv_sem=fast_sem.at[1],
-        device_id={"region": fast_peer}, device_id_type=MESH,
-    )
-
     load_wait(0)
-    mix(0)
+    mix(env.at[0])
     (start_norm,) = scalar_finish(0, 1)
     rescale = sectors * width / start_norm
 
@@ -211,29 +224,28 @@
         for k in range(slabs):
             out_slow[k, v] = value[k * rows : (k + 1) * rows]
 
-    carry_env(0, rescale, store_slow)
+    norms[0] = jnp.broadcast_to(rescale, (8, 128))
+    pair_copy(2, norms.at[0], norms.at[1]).start()
+    carry_env(frame.at[0], even, rescale, store_slow)
 
     @pl.when(inner)
     def _():
-        for k in range(AHEAD):
+        for k in range(slabs):
             slow_copy(k).start()
 
-    load_wait(1)
-    mix(1)
-
     def store_fast(v, value):
-        out_fast[v] = value
-
-    carry_env(1, rescale, store_fast)
-    fast_copy.start()
-
-    @pl.when(inner)
-    def _():
-        for k in range(AHEAD, slabs):
-            slow_copy(k).start()
+        fast[v] = value
+
+    pair_copy(0, frame.at[1], peer_frame).wait_recv()
+    pair_copy(1, left_hbm, raw).wait_recv()
+    mix(raw)
+    pair_copy(2, norms.at[0], norms.at[1]).wait_recv()
+    carry_env(peer_frame, jnp.logical_not(even), norms[1][0:1, 0:1], store_fast)
 
     @pl.when(jnp.logical_and(edge, even))
     def _():
+        load_wait(1)
+
         def body(v, carry):
             for k in range(slabs):
                 slow[k, v] = env[1, v, k * rows : (k + 1) * rows, :]
@@ -243,6 +255,8 @@
 
     @pl.when(jnp.logical_and(edge, jnp.logical_not(even)))
     def _():
+        load_wait(1)
+
         def body(v, carry):
             value = nt(unit[...], env[1, v]).astype(BF16)
             for k in range(slabs):
@@ -333,7 +347,6 @@
         value = jnp.where(keep, result[it] + diag_frame.astype(F32) * source, 0.0)
         result[it] = value
 
-    fast_copy.wait_recv()
     apply(0)
     first = result[0]
     vec[1] = first.astype(BF16)
@@ -371,7 +384,9 @@
     for which in range(3):
         for d in range(1, sectors):
             scalar_copy(which, d).wait_send()
-    fast_copy.wait_send()
+    pair_copy(0, frame.at[1], peer_frame).wait_send()
+    pair_copy(1, left_hbm, raw).wait_send()
+    pair_copy(2, norms.at[0], norms.at[1]).wait_send()
 
     @pl.when(inner)
     def _():
@@ -408,8 +423,10 @@
             pltpu.VMEM((2,) + envs, BF16),
             pltpu.VMEM(envs, BF16),
             pltpu.VMEM((2, width, width), BF16),
+            pltpu.VMEM((width, width), BF16),
+            pltpu.VMEM(envs, BF16),
+            pltpu.VMEM((2, 8, 128), F32),
             pltpu.VMEM((slabs, terms, rows, width), BF16),
-            pltpu.VMEM(envs, BF16),
             pltpu.VMEM((slabs, terms, rows, width), BF16),
             pltpu.VMEM(envs, BF16),
             pltpu.VMEM((2, width, width), BF16),
@@ -425,7 +442,8 @@
             dma((2,)),
             dma((slabs,)),
             dma((slabs,)),
-            dma((2,)),
+            dma((3,)),
+            dma((3,)),
             dma((ITERS, slabs, y_peers)),
             dma((ITERS, slabs, y_peers)),
             dma((ITERS, slabs, z_peers)),

time: 74.2 us -> 74.4 us (level)
  no operation moved by 1% of the time
where the time goes in v5:
time: 74.4 us; the launch traced here: 74.2 us
  Pallas kernels  69.5 us (93%)
  between operations  3.1 us (4%)
  local copies, waits for them, and re-layouts  1.57 us (2%)
    pallas_call x1, Pallas kernels, local(): pl.pallas_call(functools.partial(kernel, regions, ys, zs, width, terms),...  69.5 us
    unnamed x1, local copies, waits for them, and re-layouts  1.57 us

profile of v5, /device:TPU:2, one launch (start us, length us, event | category | flops | bytes accessed | tf_op | source)
XLA Modules:
  0.0 74.2 jit_solution(11093976862308018586)
XLA Ops:
  1.3 69.5 %shard_map.104 = (bf16[256,256]{1,0:T(8,128)(2,1)}, f32[1,128]{1,0:T(1,128)}) custom-call(bf16[256,256]{1,0:T(8,128)(2,1)} %bitcast.9, bf16[18,256,256]{2,1,0:T(8,128)(2,1)} %bitcast.7, bf16[18,256,256]{2,1,0:T(8,128)(2,1)} %bitcast.8, bf16[256,256]{1,0:T(8,128)(2,1)} %bitcast.10, f32[18,18]{1,0:T(8,128)} %lc_ref.1, f32[18,18]{1,0:T(8,128)} %rc_ref.1, ...), custom_call_target="tpu_custom_call" | custom-call | tf_op jit(solution)/shard_map/pallas_call | solution.py:414
  70.8 1.6 %copy.14 = bf16[1,1,256,256]{3,2,1,0:T(8,128)(2,1)} copy(bf16[1,1,256,256]{3,2,1,0:T(8,128)(2,1)} %bitcast.11) | data formatting | bytes 262144

commit v6 on v5

--- a/solution.py
+++ b/solution.py
@@ -135,7 +135,7 @@
             device_id={"region": fast_peer}, device_id_type=MESH,
         )
 
-    pair_copy(0, frame.at[1], peer_frame).start()
+    pair_copy(0, frame.at[1], peer_frame.at[0]).start()
 
     @pl.when(even)
     def _():
@@ -176,7 +176,9 @@
     hit = jnp.logical_and(aim == mine, (iota(wanted, 0) & 7) == (iota(wanted, 1) & 7))
     route[...] = jnp.where(hit, 1.0, 0.0).astype(BF16)
 
-    def mix(source):
+    def mix(source, factor):
+        right = factor[...]
+
         def body(i, carry):
             for j in range(4):
                 start = pl.multiple_of(i * 64 + j * 16, 16)
@@ -185,7 +187,8 @@
                 for h in range(2):
                     piece = x[:, 8 * h : 8 * h + 8, :].reshape(tall, width).astype(BF16)
                     halves.append(nn(matrix_mix, piece).reshape(terms, 8, width))
-                mixed[:, pl.ds(start, 16), :] = jnp.concatenate(halves, axis=1).astype(BF16)
+                both = jnp.concatenate(halves, axis=1).astype(BF16).reshape(16 * terms, width)
+                mixed[:, pl.ds(start, 16), :] = nn(both, right).astype(BF16).reshape(terms, 16, width)
             return carry
 
         lax.fori_loop(0, width // 64, body, 0)
@@ -193,17 +196,23 @@
     group = max(g for g in range(1, 10) if terms % g == 0)
 
     def carry_env(factor, ahead, rescale, store):
-        def body(i, carry):
-            for j in range(group):
-                v = i * group + j
-                a = factor[...]
-                y = nn(a, mixed[v]).astype(BF16)
-                first = jnp.where(ahead, a, y)
-                second = jnp.where(ahead, y, a)
-                store(v, (rescale * nt(first, second)).astype(BF16))
-            return carry
-
-        lax.fori_loop(0, terms // group, body, 0)
+        def run(turn):
+            def body(i, carry):
+                for j in range(group):
+                    v = i * group + j
+                    value = rescale * nn(factor[...], mixed[v])
+                    store(v, (value.T if turn else value).astype(BF16))
+                return carry
+
+            lax.fori_loop(0, terms // group, body, 0)
+
+        @pl.when(ahead)
+        def _():
+            run(True)
+
+        @pl.when(jnp.logical_not(ahead))
+        def _():
+            run(False)
 
     def load_wait(slot):
         load(left_hbm, slot).wait()
@@ -216,7 +225,7 @@
         )
 
     load_wait(0)
-    mix(env.at[0])
+    mix(env.at[0], frame.at[1])
     (start_norm,) = scalar_finish(0, 1)
     rescale = sectors * width / start_norm
 
@@ -236,11 +245,12 @@
     def store_fast(v, value):
         fast[v] = value
 
-    pair_copy(0, frame.at[1], peer_frame).wait_recv()
+    pair_copy(0, frame.at[1], peer_frame.at[0]).wait_recv()
     pair_copy(1, left_hbm, raw).wait_recv()
-    mix(raw)
+    peer_frame[1] = nt(unit[...], peer_frame[0]).astype(BF16)
+    mix(raw, peer_frame.at[1])
     pair_copy(2, norms.at[0], norms.at[1]).wait_recv()
-    carry_env(peer_frame, jnp.logical_not(even), norms[1][0:1, 0:1], store_fast)
+    carry_env(peer_frame.at[0], jnp.logical_not(even), norms[1][0:1, 0:1], store_fast)
 
     @pl.when(jnp.logical_and(edge, even))
     def _():
@@ -384,7 +394,7 @@
     for which in range(3):
         for d in range(1, sectors):
             scalar_copy(which, d).wait_send()
-    pair_copy(0, frame.at[1], peer_frame).wait_send()
+    pair_copy(0, frame.at[1], peer_frame.at[0]).wait_send()
     pair_copy(1, left_hbm, raw).wait_send()
     pair_copy(2, norms.at[0], norms.at[1]).wait_send()
 
@@ -423,7 +433,7 @@
             pltpu.VMEM((2,) + envs, BF16),
             pltpu.VMEM(envs, BF16),
             pltpu.VMEM((2, width, width), BF16),
-            pltpu.VMEM((width, width), BF16),
+            pltpu.VMEM((2, width, width), BF16),
             pltpu.VMEM(envs, BF16),
             pltpu.VMEM((2, 8, 128), F32),
             pltpu.VMEM((slabs, terms, rows, width), BF16),

time: 74.4 us -> 73.5 us (0.988)
  Pallas kernels: 69.5 us -> 68.7 us
    pallas_call x1, Pallas kernels: 69.5 us -> 68.7 us  [local(): pl.pallas_call(functools.partial(kernel, regions, ys, zs, width, terms),...]
where the time goes in v6:
time: 73.5 us; the launch traced here: 73.3 us
  Pallas kernels  68.7 us (93%)
  between operations  3.1 us (4%)
  local copies, waits for them, and re-layouts  1.57 us (2%)
    pallas_call x1, Pallas kernels, local(): pl.pallas_call(functools.partial(kernel, regions, ys, zs, width, terms),...  68.7 us
    unnamed x1, local copies, waits for them, and re-layouts  1.57 us

profile of v6, /device:TPU:2, one launch (start us, length us, event | category | flops | bytes accessed | tf_op | source)
XLA Modules:
  0.0 73.3 jit_solution(17686326601819486734)
XLA Ops:
  1.3 68.7 %shard_map.104 = (bf16[256,256]{1,0:T(8,128)(2,1)}, f32[1,128]{1,0:T(1,128)}) custom-call(bf16[256,256]{1,0:T(8,128)(2,1)} %bitcast.9, bf16[18,256,256]{2,1,0:T(8,128)(2,1)} %bitcast.7, bf16[18,256,256]{2,1,0:T(8,128)(2,1)} %bitcast.8, bf16[256,256]{1,0:T(8,128)(2,1)} %bitcast.10, f32[18,18]{1,0:T(8,128)} %lc_ref.1, f32[18,18]{1,0:T(8,128)} %rc_ref.1, ...), custom_call_target="tpu_custom_call" | custom-call | tf_op jit(solution)/shard_map/pallas_call | solution.py:424
  69.9 1.6 %copy.14 = bf16[1,1,256,256]{3,2,1,0:T(8,128)(2,1)} copy(bf16[1,1,256,256]{3,2,1,0:T(8,128)(2,1)} %bitcast.11) | data formatting | bytes 262144

commit v7 on v6

--- a/solution.py
+++ b/solution.py
@@ -154,9 +154,9 @@
             load(right_hbm, 1).start()
 
 
-    tall = 8 * terms
-    spread = jnp.where((iota((tall, terms), 0) >> 3) == iota((tall, terms), 1), 1.0, 0.0).astype(BF16)
-    same = (iota((tall, tall), 0) & 7) == (iota((tall, tall), 1) & 7)
+    tall = 16 * terms
+    spread = jnp.where((iota((tall, terms), 0) >> 4) == iota((tall, terms), 1), 1.0, 0.0).astype(BF16)
+    same = (iota((tall, tall), 0) & 15) == (iota((tall, tall), 1) & 15)
     pattern = mask_ref[...].astype(F32)
 
     def mixer(coeff):
@@ -166,14 +166,14 @@
     left_c, right_c = lc_ref[...], rc_ref[...]
     parity = odd.astype(F32)
     matrix_mix = mixer(right_c + parity * (left_c - right_c))
-    wanted = (sectors * 8, tall)
+    wanted = (sectors * 16, tall)
     aim = jnp.zeros(wanted, jnp.int32)
     for w in range(terms):
-        aim = jnp.where((iota(wanted, 1) >> 3) == w, target_ref[0, w], aim)
-    block = iota(wanted, 0) >> 3
+        aim = jnp.where((iota(wanted, 1) >> 4) == w, target_ref[0, w], aim)
+    block = iota(wanted, 0) >> 4
     z_bits = zs.bit_length() - 1
     mine = (block & (zs - 1)) * ys + (block >> z_bits)
-    hit = jnp.logical_and(aim == mine, (iota(wanted, 0) & 7) == (iota(wanted, 1) & 7))
+    hit = jnp.logical_and(aim == mine, (iota(wanted, 0) & 15) == (iota(wanted, 1) & 15))
     route[...] = jnp.where(hit, 1.0, 0.0).astype(BF16)
 
     def mix(source, factor):
@@ -182,12 +182,8 @@
         def body(i, carry):
             for j in range(4):
                 start = pl.multiple_of(i * 64 + j * 16, 16)
-                x = source[:, pl.ds(start, 16), :].astype(F32)
-                halves = []
-                for h in range(2):
-                    piece = x[:, 8 * h : 8 * h + 8, :].reshape(tall, width).astype(BF16)
-                    halves.append(nn(matrix_mix, piece).reshape(terms, 8, width))
-                both = jnp.concatenate(halves, axis=1).astype(BF16).reshape(16 * terms, width)
+                piece = source[:, pl.ds(start, 16), :].reshape(tall, width)
+                both = nn(matrix_mix, piece).astype(BF16)
                 mixed[:, pl.ds(start, 16), :] = nn(both, right).astype(BF16).reshape(terms, 16, width)
             return carry
 
@@ -324,15 +320,11 @@
                 pieces = [
                     half[(j * terms + w) * rows : (j * terms + w + 1) * rows] for j in range(merge)
                 ]
-                term[w, 0:tile, :] = nn(jnp.concatenate(pieces, axis=0), fast[w])
+                term[w, 0:tile, :] = nn(jnp.concatenate(pieces, axis=0), fast[w]).astype(BF16)
             matrix = route[...]
             for i in range(tile // 16):
-                halves = []
-                for h in range(2):
-                    at = 16 * i + 8 * h
-                    piece = term[:, at : at + 8, :].reshape(tall, width).astype(BF16)
-                    halves.append((nn(matrix, piece) * inv_root).reshape(ys, zs, 8, width))
-                both = jnp.concatenate(halves, axis=2).astype(BF16)
+                piece = term[:, 16 * i : 16 * i + 16, :].reshape(tall, width)
+                both = (nn(matrix, piece) * inv_root).astype(BF16).reshape(ys, zs, 16, width)
                 part[it][k, :, :, 16 * i : 16 * i + 16, :] = both
             for d in range(1, ys):
                 y_copy(it, k, d).start()
@@ -441,8 +433,8 @@
             pltpu.VMEM(envs, BF16),
             pltpu.VMEM((2, width, width), BF16),
             pltpu.VMEM((width, width), BF16),
-            pltpu.VMEM((sectors * 8, terms * 8), BF16),
-            pltpu.VMEM((terms, max(tiles), width), F32),
+            pltpu.VMEM((sectors * 16, terms * 16), BF16),
+            pltpu.VMEM((terms, max(tiles), width), BF16),
             *[pltpu.VMEM((n, ys, zs, width // n, width), BF16) for n in SLABS],
             *[pltpu.VMEM((n, y_peers, zs, width // n, width), BF16) for n in SLABS],
             *[pltpu.VMEM((n, zs, width // n, width), BF16) for n in SLABS],

time: 73.5 us -> 76.2 us (1.037)
  Pallas kernels: 68.7 us -> 71.4 us
    pallas_call x1, Pallas kernels: 68.7 us -> 71.4 us  [local(): pl.pallas_call(functools.partial(kernel, regions, ys, zs, width, terms),...]
where the time goes in v7:
time: 76.2 us; the launch traced here: 76 us
  Pallas kernels  71.4 us (94%)
  between operations  3.1 us (4%)
  local copies, waits for them, and re-layouts  1.57 us (2%)
    pallas_call x1, Pallas kernels, local(): pl.pallas_call(functools.partial(kernel, regions, ys, zs, width, terms),...  71.4 us
    unnamed x1, local copies, waits for them, and re-layouts  1.57 us

profile of v7, /device:TPU:2, one launch (start us, length us, event | category | flops | bytes accessed | tf_op | source)
XLA Modules:
  0.0 76.0 jit_solution(7922415780466761543)
XLA Ops:
  1.3 71.4 %shard_map.104 = (bf16[256,256]{1,0:T(8,128)(2,1)}, f32[1,128]{1,0:T(1,128)}) custom-call(bf16[256,256]{1,0:T(8,128)(2,1)} %bitcast.9, bf16[18,256,256]{2,1,0:T(8,128)(2,1)} %bitcast.7, bf16[18,256,256]{2,1,0:T(8,128)(2,1)} %bitcast.8, bf16[256,256]{1,0:T(8,128)(2,1)} %bitcast.10, f32[18,18]{1,0:T(8,128)} %lc_ref.1, f32[18,18]{1,0:T(8,128)} %rc_ref.1, ...), custom_call_target="tpu_custom_call" | custom-call | tf_op jit(solution)/shard_map/pallas_call | solution.py:416
  72.7 1.6 %copy.14 = bf16[1,1,256,256]{3,2,1,0:T(8,128)(2,1)} copy(bf16[1,1,256,256]{3,2,1,0:T(8,128)(2,1)} %bitcast.11) | data formatting | bytes 262144
